TPU v7x, 256 devices: a whole 4x4x8 slice. The times are simulated.
256 devices in a mesh: ctx: 16 (over y_hi, x, core), exp: 8 (over z), dp: 2 (over y_lo).
Axes of the slice: x: 4, y: 4 (y_hi: 2, y_lo: 2; y = y_hi * 2 + y_lo), z: 8, core: 2. Of those that a mesh axis runs over, the one named last changes fastest.
Arguments:
- tokens: bfloat16 [2, 2048, 4096], P('dp', 'ctx'), may hold values from -6 to 6
- norm_in: bfloat16 [4096], replicated, may hold values from 0.099609375 to 1.8984375
- w_qkv: bfloat16 [4096, 8, 6, 128], P('dp', 'exp')
- w_out: bfloat16 [8, 4, 128, 4096], P('exp', None, None, 'dp'), may hold values from -0.375 to 0.375
- norm_mid: bfloat16 [4096], replicated, may hold values from 0.099609375 to 1.8984375
- w_router: bfloat16 [4096, 8], replicated, may hold values from -0.09375 to 0.09375
- w_gate_up: bfloat16 [8, 4096, 2, 8192], P('exp', 'dp', None, 'ctx'), may hold values from -0.09375 to 0.09375
- w_down: bfloat16 [8, 8192, 4096], P('exp', 'ctx', 'dp'), may hold values from -0.0625 to 0.0625
- expert_ids: int32 [2, 2048, 2], P('dp', ('ctx', 'exp')), may hold values from 0 to 7, as said below
- slot_index: int32 [2, 2048, 2], P('dp', ('ctx', 'exp')), may hold values from 0 to 5, as said below
Outputs:
- layer_out: bfloat16 [2, 2048, 4096], P('dp', ('ctx', 'exp'))
Inputs may be any that keep to these rules, and one draw needn't show every extreme that they name: `expert_ids`: each token names two different experts; in every aligned block of 16 tokens (the tokens of one device) the numbers of choices of the experts are, in some order, 6, 5, 4, 4, 4, 3, 3 and 3, so that no expert is named more than 6 times and one exactly 6 times. `slot_index`: a choice's slot is the number of earlier choices of the same expert in its block of 16 tokens, a token's first choice counting before its second.
All inputs are finite; a program needn't handle non-finite values.
Results may differ from a plain program's by a relative error of at most 0.022.
The roundings to bfloat16 on the way count: a program that leaves them out, or rounds other values in their place, can miss the bound.
Values may be sent and summed in bfloat16 or wider, within the bound.
No kernel may reach another device: no remote copies, remote signals or barrier semaphores. Data moves between devices by JAX's collectives and lax.ppermute only.
A program may use at most 128 MiB of HBM per device.

v0:
```python
import math
import jax
import jax.numpy as jnp
from jax import lax
from jax.sharding import PartitionSpec as P

EPSILON = 1e-05
ROPE_BASE = 1000000.0


def rms_norm(values, gain):
    wide = values.astype(jnp.float32)
    square_mean = jnp.mean(wide * wide, axis=-1, keepdims=True)
    return (wide * lax.rsqrt(square_mean + EPSILON) * gain.astype(jnp.float32)).astype(jnp.bfloat16)


def rope_angles(positions, head_dim):
    half_dim = head_dim // 2
    freqs = jnp.exp(
        jnp.arange(half_dim, dtype=jnp.float32) * (-2.0 * math.log(ROPE_BASE) / head_dim)
    )
    return positions[:, None] * freqs[None, :]


def rotate(tensor, angles):
    half_dim = tensor.shape[-1] // 2
    first_half = tensor[..., :half_dim]
    second_half = tensor[..., half_dim:]
    cosine = jnp.cos(angles)
    sine = jnp.sin(angles)
    return jnp.concatenate(
        [first_half * cosine - second_half * sine, second_half * cosine + first_half * sine],
        axis=-1,
    )


def on_device(
    tokens, norm_in, w_qkv, w_out, norm_mid, w_router, w_gate_up, w_down, expert_ids, slot_index
):
    tok_rows = tokens.shape[1]
    head_dim = w_qkv.shape[3]
    kv_local = w_qkv.shape[1]
    group_size = w_qkv.shape[2] - 2
    width = tokens.shape[2]
    normed = rms_norm(tokens, norm_in)
    qkv_full, out_full, gate_up_all, down_all = (
        lax.all_gather(w_qkv, "dp", axis=0, tiled=True),
        lax.all_gather(w_out, "dp", axis=3, tiled=True),
        lax.all_gather(w_gate_up, "dp", axis=1, tiled=True),
        lax.all_gather(w_down, "dp", axis=2, tiled=True),
    )
    projected = jnp.dot(normed[0], qkv_full.reshape(width, -1), preferred_element_type=jnp.float32)[
        None
    ]
    projected = projected.reshape(1, tok_rows, kv_local, group_size + 2, head_dim)
    query_idx = lax.axis_index("ctx") * tok_rows + jnp.arange(tok_rows, dtype=jnp.int32)
    angles = rope_angles(query_idx.astype(jnp.float32), head_dim)
    queries = rotate(projected[:, :, :, :group_size, :], angles[None, :, None, None, :]).astype(
        jnp.bfloat16
    )
    keys_rot = rotate(projected[:, :, :, group_size, :], angles[None, :, None, :]).astype(
        jnp.bfloat16
    )
    values = projected[:, :, :, group_size + 1, :].astype(jnp.bfloat16)
    scale = 1.0 / math.sqrt(head_dim)
    last_query = lax.axis_index("ctx") * tok_rows + tok_rows - 1
    peak_init = jnp.full((1, kv_local, group_size, tok_rows), -1e30, jnp.float32)
    total_init = jnp.zeros((1, kv_local, group_size, tok_rows), jnp.float32)
    accum_init = jnp.zeros((1, kv_local, group_size, tok_rows, head_dim), jnp.float32)
    key_piece = lax.all_gather(keys_rot, "ctx", axis=1, tiled=True)
    value_piece = lax.all_gather(values, "ctx", axis=1, tiled=True)
    count = key_piece.shape[1]

    def compute(state):
        peak, totals, accum = state
        score_matrix = (
            jnp.einsum("bqkgd,bskd->bkgqs", queries, key_piece, preferred_element_type=jnp.float32)
            * scale
        )
        key_idx = jnp.arange(count, dtype=jnp.int32)
        causal = key_idx[None, :] <= query_idx[:, None]
        score_matrix = jnp.where(causal, score_matrix, -1e30)
        new_peak = jnp.maximum(peak, jnp.max(score_matrix, axis=-1))
        probs = jnp.where(causal, jnp.exp(score_matrix - new_peak[..., None]), 0.0)
        totals = jnp.sum(probs, axis=-1)
        update = jnp.einsum(
            "bkgqs,bskd->bkgqd",
            probs.astype(jnp.bfloat16),
            value_piece,
            preferred_element_type=jnp.float32,
        )
        accum = update
        return (new_peak, totals, accum)

    peak, totals, accum = lax.cond(
        jnp.int32(0) <= last_query,
        compute,
        lambda state: state,
        (peak_init, total_init, accum_init),
    )
    attended = jnp.transpose(accum / totals[..., None], (0, 3, 1, 2, 4)).astype(jnp.bfloat16)
    attended = attended.reshape(1, tok_rows, kv_local * group_size * head_dim)
    partial_sum = jnp.dot(
        attended[0], out_full.reshape(-1, width), preferred_element_type=jnp.float32
    )[None]
    head_total = lax.psum_scatter(
        partial_sum.astype(jnp.bfloat16), "exp", scatter_dimension=1, tiled=True
    ).astype(jnp.float32)
    rows = head_total.shape[1]
    own_tokens = lax.dynamic_slice_in_dim(tokens, lax.axis_index("exp") * rows, rows, 1)
    mixed = (own_tokens[0].astype(jnp.float32) + head_total[0]).astype(jnp.bfloat16)
    normed_mid = rms_norm(mixed, norm_mid)
    expert_count = w_router.shape[1]
    logits = jnp.dot(normed_mid, w_router, preferred_element_type=jnp.float32)
    choice_ids = expert_ids[0]
    picks = choice_ids[:, :, None] == jnp.arange(expert_count, dtype=jnp.int32)[None, None, :]
    chosen = jnp.sum(jnp.where(picks, logits[:, None, :], 0.0), axis=-1)
    gate_first = 1.0 / (1.0 + jnp.exp(chosen[:, 1] - chosen[:, 0]))
    gate_second = 1.0 - gate_first
    capacity = 6 * (rows // 16)
    exp_count = lax.axis_size("exp")
    exp_local = gate_up_all.shape[0]
    flat_index = choice_ids * capacity + slot_index[0]
    slot_cols = jnp.arange(expert_count * capacity, dtype=jnp.int32)
    placer = jnp.logical_or(
        slot_cols[:, None] == flat_index[None, :, 0], slot_cols[:, None] == flat_index[None, :, 1]
    ).astype(jnp.bfloat16)
    buffer_rows = jnp.dot(placer, normed_mid, preferred_element_type=jnp.float32).astype(
        jnp.bfloat16
    )
    buffer_rows = buffer_rows.reshape(exp_count, exp_local, capacity, width)
    received = lax.all_to_all(buffer_rows, "exp", split_axis=0, concat_axis=0, tiled=True)
    gathered_rows = lax.all_gather(received[None], "ctx", axis=0, tiled=True)
    gate_up_vals = jnp.einsum(
        "cnlrd,ldjf->cnlrjf", gathered_rows, gate_up_all, preferred_element_type=jnp.float32
    )
    hidden = (jax.nn.silu(gate_up_vals[..., 0, :]) * gate_up_vals[..., 1, :]).astype(jnp.bfloat16)
    summed_result = lax.psum_scatter(
        jnp.einsum("cnlrf,lfd->cnlrd", hidden, down_all, preferred_element_type=jnp.float32).astype(
            jnp.bfloat16
        ),
        "ctx",
        scatter_dimension=0,
        tiled=True,
    ).astype(jnp.float32)
    expert_out = summed_result[0].astype(jnp.bfloat16)
    returned = lax.all_to_all(expert_out, "exp", split_axis=0, concat_axis=0, tiled=True)
    returned = returned.reshape(expert_count * capacity, width)
    combiner = gate_first[:, None] * (flat_index[:, 0:1] == slot_cols[None, :]).astype(
        jnp.float32
    ) + gate_second[:, None] * (flat_index[:, 1:2] == slot_cols[None, :]).astype(jnp.float32)
    moe_total = jnp.dot(combiner, returned.astype(jnp.float32), precision=lax.Precision.HIGHEST)
    return (mixed.astype(jnp.float32) + moe_total).astype(jnp.bfloat16)[None]


def solution(mesh):
    placed = (
        P("dp", "ctx", None),
        P(),
        P("dp", "exp", None, None),
        P("exp", None, None, "dp"),
        P(),
        P(),
        P("exp", "dp", None, "ctx"),
        P("exp", "ctx", "dp"),
        P("dp", ("ctx", "exp"), None),
        P("dp", ("ctx", "exp"), None),
    )
    return jax.shard_map(
        on_device,
        mesh=mesh,
        in_specs=placed,
        out_specs=P("dp", ("ctx", "exp"), None),
        check_vma=False,
    )
```

profile of v0, /device:TPU:2, one launch (start us, length us, event | category | flops | bytes accessed | tf_op | source)
XLA Modules:
  0.0 595.8 jit_solution(7468417833645752006)
XLA Ops:
  6.5 4.8 copy.44
  13.1 86.9 %all-gather.8.cloned.1.call-done = bf16[4096,1,6,128]{0,3,2,1:T(8,128)(2,1)} async-done(((bf16[2048,1,6,128]{0,3,2,1:T(8,128)(2,1)}), bf16[4096,1,6,128]{0,3,2,1:T(8,128)(2,1)}) %all-gather.8.cloned.1.call-update) | async-done | bytes 6291472 | tf_op jit(solution)/shard_map/all_gather | solution.py:47
  99.9 4.6 fusion.36
  104.9 21.1 %all_gather.22 = bf16[1,2048,1,128]{1,3,2,0:T(8,128)(2,1)S(1)} all-gather(bf16[1,128,1,128]{1,3,2,0:T(8,128)(2,1)S(1)} %pad_maximum_fusion.1), channel_id=1, replica_groups=mesh['ctx'=16,'exp'=8,'dp'=2] {'ctx'}, dimensions={1}, use_global_device_ids=true | all-gather | bytes 557056 | tf_op jit(solution)/shard_map/all_gather | solution.py:70
  126.0 25.5 %all-gather = bf16[1,2048,1,1,128]{1,4,3,2,0:T(8,128)(2,1)S(1)} all-gather(bf16[1,128,1,1,128]{1,4,3,2,0:T(8,128)(2,1)S(1)} %slice.86), channel_id=2, replica_groups=mesh['ctx'=16,'exp'=8,'dp'=2] {'ctx'}, dimensions={1}, use_global_device_ids=true | all-gather | bytes 557056 | tf_op jit(solution)/shard_map/all_gather | solution.py:71
  151.4 3.1 conditional.1
  152.4 1.1 fusion.7
  153.5 1.0 fusion.2
  154.5 10.0 %all-gather.10.cloned.1.call-done = bf16[1,4,128,4096]{3,2,1,0:T(8,128)(2,1)} async-done(((bf16[1,4,128,2048]{3,2,1,0:T(8,128)(2,1)}), bf16[1,4,128,4096]{3,2,1,0:T(8,128)(2,1)}) %all-gather.10.cloned.1.call-update) | async-done | bytes 4194320 | tf_op jit(solution)/shard_map/all_gather | solution.py:48
  164.6 3.9 fusion.23
  168.6 4.9 copy.51
  174.2 36.3 %reduce-scatter.3.cloned.1.call-done = bf16[1,16,4096]{2,1,0:T(8,128)(2,1)} async-done(((bf16[1,128,4096]{2,1,0:T(8,128)(2,1)}), bf16[1,16,4096]{2,1,0:T(8,128)(2,1)}) %reduce-scatter.3.cloned.1.call-update) | async-done | bytes 131088 | tf_op jit(solution)/shard_map/reduce_scatter | solution.py:106
  210.5 1.1 fusion.45
  212.0 17.6 %all_to_all.10 = bf16[8,1,6,4096]{3,2,1,0:T(8,128)(2,1)S(1)} all-to-all(bf16[8,1,6,4096]{3,2,1,0:T(8,128)(2,1)S(1)} %bitcast.132), channel_id=1, replica_groups=mesh['ctx'=16,'exp'=8,'dp'=2] {'exp'}, dimensions={0} | all-to-all | bytes 786432 | tf_op jit(solution)/shard_map/all_to_all | solution.py:132
  231.4 88.6 %all-gather.12.cloned.1.call-done = bf16[1,4096,2,512]{3,1,2,0:T(8,128)(2,1)} async-done(((bf16[1,2048,2,512]{3,1,2,0:T(8,128)(2,1)}), bf16[1,4096,2,512]{3,1,2,0:T(8,128)(2,1)}) %all-gather.12.cloned.1.call-update) | async-done | bytes 8388624 | tf_op jit(solution)/shard_map/all_gather | solution.py:49
  320.0 72.3 %all-gather.16.cloned.1.call-done = bf16[128,1,6,4096]{3,0,2,1:T(8,128)(2,1)} async-done(((bf16[8,1,6,4096]{3,0,2,1:T(8,128)(2,1)}), bf16[128,1,6,4096]{3,0,2,1:T(8,128)(2,1)}) %all-gather.16.cloned.1.call-update) | async-done | bytes 6291472 | tf_op jit(solution)/shard_map/all_gather | solution.py:133
  392.3 12.1 %fusion.30 = f32[16,8,1,6,2,512]{5,1,4,3,0,2:T(8,128)} fusion(bf16[1,4096,2,512]{3,1,2,0:T(8,128)(2,1)} %all-gather.12.cloned.1.call-done, bf16[128,1,6,4096]{3,0,2,1:T(8,128)(2,1)} %all-gather.16.cloned.1.call-done), kind=kOutput, calls=%fused_computation.38 | convolution fusion | flops 6442450944 | bytes 17825792 | tf_op jit(solution)/shard_map/cnlrd,ldjf->cnlrjf/dot_general | solution.py:134
  404.4 50.6 %all-gather.14.cloned.1.call-done = bf16[1,512,4096]{2,1,0:T(8,128)(2,1)} async-done(((bf16[1,512,2048]{2,1,0:T(8,128)(2,1)}), bf16[1,512,4096]{2,1,0:T(8,128)(2,1)}) %all-gather.14.cloned.1.call-update) | async-done | bytes 4194320 | tf_op jit(solution)/shard_map/all_gather | solution.py:50
  455.0 9.2 %fusion.22 = bf16[16,8,1,6,4096]{4,1,3,0,2:T(8,128)(2,1)} fusion(bf16[1,512,4096]{2,1,0:T(8,128)(2,1)} %all-gather.14.cloned.1.call-done, f32[16,8,1,6,2,512]{5,1,4,3,0,2:T(8,128)} %fusion.30), kind=kOutput, calls=%fused_computation.25 | convolution fusion | flops 3226730496 | bytes 13631488 | tf_op jit(solution)/shard_map/cnlrf,lfd->cnlrd/dot_general | solution.py:139
  464.3 98.2 %reduce-scatter.5.cloned.1.call-done = bf16[1,8,1,6,4096]{4,1,3,0,2:T(8,128)(2,1)} async-done(((bf16[16,8,1,6,4096]{4,1,3,0,2:T(8,128)(2,1)}), bf16[1,8,1,6,4096]{4,1,3,0,2:T(8,128)(2,1)}) %reduce-scatter.5.cloned.1.call-update) | async-done | bytes 393232 | tf_op jit(solution)/shard_map/reduce_scatter | solution.py:138
  562.5 2.0 copy.53
  564.5 7.0 %all-to-all-start.1 = ((bf16[8,1,6,4096]{3,2,1,0:T(8,128)(2,1)}), bf16[8,1,6,4096]{3,2,1,0:T(8,128)(2,1)S(1)}, u32[]{:S(2)}, u32[]{:S(2)}) async-start(bf16[8,1,6,4096]{3,2,1,0:T(8,128)(2,1)} %copy.53), calls=%async_computation.3 | async-start | bytes 1048576 | tf_op jit(solution)/shard_map/all_to_all | solution.py:147
  571.8 16.1 %all-to-all-done.1 = bf16[8,1,6,4096]{3,2,1,0:T(8,128)(2,1)S(1)} async-done(((bf16[8,1,6,4096]{3,2,1,0:T(8,128)(2,1)}), bf16[8,1,6,4096]{3,2,1,0:T(8,128)(2,1)S(1)}, u32[]{:S(2)}, u32[]{:S(2)}) %all-to-all-start.1) | async-done | bytes 393248 | tf_op jit(solution)/shard_map/all_to_all | solution.py:147
  588.0 1.0 fusion.25
  (55 shorter events, 6.4 us)
Async XLA Ops:
  6.5 565.0 %copy-start = (bf16[4096,8]{0,1:T(8,128)(2,1)S(1)}, bf16[4096,8]{0,1:T(8,128)(2,1)}, u32[]{:S(2)}) copy-start(bf16[4096,8]{0,1:T(8,128)(2,1)} %param.17) | copy-start | bytes 196612
  6.5 93.4 %all-gather.8.cloned.1.call-start = ((), (), s32[]{:S(2)}) async-start(), calls=%async_computation.4 | async-start | bytes 9437184 | tf_op jit(solution)/shard_map/all_gather | solution.py:47
  11.3 0.8 copy-start.2
  11.3 1.2 copy-start.1
  11.3 153.2 %all-gather.10.cloned.1.call-start = ((), (), s32[]{:S(2)}) async-start(), calls=%async_computation.5 | async-start | bytes 6291456 | tf_op jit(solution)/shard_map/all_gather | solution.py:48
  12.1 198.4 %reduce-scatter.3.cloned.1.call-start = ((), (), s32[]{:S(2)}) async-start(), calls=%async_computation.6 | async-start | bytes 1179648 | tf_op jit(solution)/shard_map/reduce_scatter | solution.py:106
  168.5 151.5 %all-gather.12.cloned.1.call-start = ((), (), s32[]{:S(2)}) async-start(), calls=%async_computation.7 | async-start | bytes 12582912 | tf_op jit(solution)/shard_map/all_gather | solution.py:49
  173.5 0.7 copy-start.3
  173.5 0.7 copy-start.4
  173.5 0.7 copy-start.5
  173.5 218.9 %all-gather.16.cloned.1.call-start = ((), (), s32[]{:S(2)}) async-start(), calls=%async_computation.10 | async-start | bytes 6684672 | tf_op jit(solution)/shard_map/all_gather | solution.py:133
  230.6 224.4 %all-gather.14.cloned.1.call-start = ((), (), s32[]{:S(2)}) async-start(), calls=%async_computation.8 | async-start | bytes 6291456 | tf_op jit(solution)/shard_map/all_gather | solution.py:50
  231.2 331.3 %reduce-scatter.5.cloned.1.call-start = ((), (), s32[]{:S(2)}) async-start(), calls=%async_computation.9 | async-start | bytes 6684672 | tf_op jit(solution)/shard_map/reduce_scatter | solution.py:138
  564.5 23.4 %all-to-all-start.1 = ((bf16[8,1,6,4096]{3,2,1,0:T(8,128)(2,1)}), bf16[8,1,6,4096]{3,2,1,0:T(8,128)(2,1)S(1)}, u32[]{:S(2)}, u32[]{:S(2)}) async-start(bf16[8,1,6,4096]{3,2,1,0:T(8,128)(2,1)} %copy.53), calls=%async_computation.3 | async-start | bytes 1048576 | tf_op jit(solution)/shard_map/all_to_all | solution.py:147
Sparse Core Ops, SparseCore 0:
  11.5 88.4 all-gather.7
  101.7 62.8 all-gather.9
  168.6 41.8 reduce-scatter.2
  212.2 107.8 all-gather.11
  322.7 69.6 all-gather.15
  394.0 60.9 all-gather.13
  464.4 98.0 reduce-scatter.4
where the time goes:
time: 596 us
  waiting for transfers between devices  460 us (77%)
  blocking collectives  64.1 us (11%)
  matrix products  33.3 us (6%)
  local copies, waits for them, and re-layouts  14 us (2%)
  between operations  13.7 us (2%)
  starting transfers between devices  7.44 us (1%)
    reduce_scatter x1, waiting for transfers between devices, on_device(): lax.psum_scatter(jnp.einsum('cnlrf,lfd->cnlrd', hidden, down_all, preferr...  98.2 us
    all_gather x1, waiting for transfers between devices, on_device(): lax.all_gather(w_gate_up, 'dp', axis=1, tiled=True)  88.6 us
    all_gather x1, waiting for transfers between devices, on_device(): lax.all_gather(w_qkv, 'dp', axis=0, tiled=True)  86.9 us
    all_gather x1, waiting for transfers between devices, on_device(): gathered_rows = lax.all_gather(received[None], 'ctx', axis=0, tiled=True)  72.3 us
    all_gather x1, waiting for transfers between devices, on_device(): lax.all_gather(w_down, 'dp', axis=2, tiled=True)  50.6 us
    reduce_scatter x1, waiting for transfers between devices, on_device(): lax.psum_scatter(partial_sum.astype(jnp.bfloat16), 'exp', scatter_dimensi...  36.3 us
    all_gather x1, blocking collectives, on_device(): value_piece = lax.all_gather(values, 'ctx', axis=1, tiled=True)  25.5 us
    all_gather x1, blocking collectives, on_device(): key_piece = lax.all_gather(keys_rot, 'ctx', axis=1, tiled=True)  21.1 us
  transfers between devices with their start and end apart: 8, of which 8 were waited for; matrix products, arithmetic and copies ran while one was open for 5% of the time, Pallas kernels for 0%

commit v1 on v0

--- a/solution.py
+++ b/solution.py
@@ -46,7 +46,9 @@
     qkv_full, out_full, gate_up_all, down_all = (
         lax.all_gather(w_qkv, "dp", axis=0, tiled=True),
         lax.all_gather(w_out, "dp", axis=3, tiled=True),
-        lax.all_gather(w_gate_up, "dp", axis=1, tiled=True),
+        jnp.concatenate(
+            lax.all_to_all(jnp.stack([w_gate_up] * lax.axis_size("dp")), "dp", 0, 0), axis=1
+        ),
         lax.all_gather(w_down, "dp", axis=2, tiled=True),
     )
     projected = jnp.dot(normed[0], qkv_full.reshape(width, -1), preferred_element_type=jnp.float32)[

time: 596 us -> 544 us (0.913)
  waiting for transfers between devices: 460 us -> 384 us
  other arithmetic: 3.13 us -> 18.5 us
  starting transfers between devices: 7.44 us -> 14.4 us
    all_to_all x0 -> x1, waiting for transfers between devices: none -> 135 us  [on_device(): lax.all_to_all(jnp.stack([w_gate_up] * lax.axis_size('dp')), 'dp', 0, 0)]
    all_gather x1 -> x0, waiting for transfers between devices: 88.6 us -> none  [on_device(): lax.all_gather(w_gate_up, 'dp', axis=1, tiled=True)]
    all_gather x1, waiting for transfers between devices: 72.3 us -> 0.01 us  [on_device(): gathered_rows = lax.all_gather(received[None], 'ctx', axis=0, tiled=True)]
    all_gather x1, waiting for transfers between devices: 50.6 us -> 0.02 us  [on_device(): lax.all_gather(w_down, 'dp', axis=2, tiled=True)]
    another operation x2 -> x3, other arithmetic: 0.25 us -> 15.2 us  [the longest x1 14.9 us: on_device(): jnp.stack([w_gate_up] * lax.axis_size('dp'))]
    all_to_all x0 -> x1, local copies, waits for them, and re-layouts: none -> 8.03 us  [on_device(): lax.all_to_all(jnp.stack([w_gate_up] * lax.axis_size('dp')), 'dp', 0, 0)]
    all_to_all x0 -> x1, starting transfers between devices: none -> 6.99 us  [on_device(): lax.all_to_all(jnp.stack([w_gate_up] * lax.axis_size('dp')), 'dp', 0, 0)]
  transfers between devices with their start and end apart: 8 -> 8, of which waited for: 8 -> 6; matrix products, arithmetic and copies ran while one was open for 5% -> 8% of each run, Pallas kernels for 0% -> 0%
where the time goes in v1:
time: 544 us; the launch traced here: 543 us
  waiting for transfers between devices  384 us (71%)
  blocking collectives  64.2 us (12%)
  matrix products  31.5 us (6%)
  other arithmetic  18.5 us (3%)
  local copies, waits for them, and re-layouts  16.5 us (3%)
  starting transfers between devices  14.4 us (3%)
  between operations  13.7 us (3%)
    all_to_all x1, waiting for transfers between devices, on_device(): lax.all_to_all(jnp.stack([w_gate_up] * lax.axis_size('dp')), 'dp', 0, 0)  135 us
    reduce_scatter x1, waiting for transfers between devices, on_device(): lax.psum_scatter(jnp.einsum('cnlrf,lfd->cnlrd', hidden, down_all, preferr...  93.7 us
    all_gather x1, waiting for transfers between devices, on_device(): lax.all_gather(w_qkv, 'dp', axis=0, tiled=True)  86.9 us
    reduce_scatter x1, waiting for transfers between devices, on_device(): lax.psum_scatter(partial_sum.astype(jnp.bfloat16), 'exp', scatter_dimensi...  41.8 us
    all_gather x1, blocking collectives, on_device(): value_piece = lax.all_gather(values, 'ctx', axis=1, tiled=True)  25.5 us
    all_gather x1, blocking collectives, on_device(): key_piece = lax.all_gather(keys_rot, 'ctx', axis=1, tiled=True)  21.1 us
    all_to_all x1, blocking collectives, on_device(): lax.all_to_all(buffer_rows, 'exp', split_axis=0, concat_axis=0, tiled=True)  17.6 us
    all_to_all x1, waiting for transfers between devices, on_device(): lax.all_to_all(expert_out, 'exp', split_axis=0, concat_axis=0, tiled=True)  16.1 us
  transfers between devices with their start and end apart: 8, of which 6 were waited for; matrix products, arithmetic and copies ran while one was open for 8% of the time, Pallas kernels for 0%

profile of v1, /device:TPU:2, one launch (start us, length us, event | category | flops | bytes accessed | tf_op | source)
XLA Modules:
  0.0 543.3 jit_solution(11214517699658628318)
XLA Ops:
  6.5 4.8 copy.47
  13.1 86.9 %all-gather.7.cloned.1.call-done = bf16[4096,1,6,128]{0,3,2,1:T(8,128)(2,1)} async-done(((bf16[2048,1,6,128]{0,3,2,1:T(8,128)(2,1)}), bf16[4096,1,6,128]{0,3,2,1:T(8,128)(2,1)}) %all-gather.7.cloned.1.call-update) | async-done | bytes 6291472 | tf_op jit(solution)/shard_map/all_gather | solution.py:47
  99.9 4.6 fusion.34
  104.9 21.1 %all_gather.19 = bf16[1,2048,1,128]{1,3,2,0:T(8,128)(2,1)S(1)} all-gather(bf16[1,128,1,128]{1,3,2,0:T(8,128)(2,1)S(1)} %pad_maximum_fusion.2), channel_id=1, replica_groups=mesh['ctx'=16,'exp'=8,'dp'=2] {'ctx'}, dimensions={1}, use_global_device_ids=true | all-gather | bytes 557056 | tf_op jit(solution)/shard_map/all_gather | solution.py:72
  126.0 25.5 %all-gather = bf16[1,2048,1,1,128]{1,4,3,2,0:T(8,128)(2,1)S(1)} all-gather(bf16[1,128,1,1,128]{1,4,3,2,0:T(8,128)(2,1)S(1)} %slice.84), channel_id=2, replica_groups=mesh['ctx'=16,'exp'=8,'dp'=2] {'ctx'}, dimensions={1}, use_global_device_ids=true | all-gather | bytes 557056 | tf_op jit(solution)/shard_map/all_gather | solution.py:73
  151.5 3.1 conditional.1
  152.4 1.0 fusion.2
  153.5 1.0 fusion.7
  154.6 10.0 %all-gather.9.cloned.1.call-done = bf16[1,4,128,4096]{3,2,1,0:T(8,128)(2,1)} async-done(((bf16[1,4,128,2048]{3,2,1,0:T(8,128)(2,1)}), bf16[1,4,128,4096]{3,2,1,0:T(8,128)(2,1)}) %all-gather.9.cloned.1.call-update) | async-done | bytes 4194320 | tf_op jit(solution)/shard_map/all_gather | solution.py:48
  164.6 3.9 fusion.23
  168.7 41.8 %reduce-scatter.3.cloned.1.call-done = bf16[1,16,4096]{2,1,0:T(8,128)(2,1)} async-done(((bf16[1,128,4096]{2,1,0:T(8,128)(2,1)}), bf16[1,16,4096]{2,1,0:T(8,128)(2,1)}) %reduce-scatter.3.cloned.1.call-update) | async-done | bytes 131088 | tf_op jit(solution)/shard_map/reduce_scatter | solution.py:108
  210.5 1.1 fusion.43
  212.0 17.6 %all_to_all.15 = bf16[8,1,6,4096]{3,2,1,0:T(8,128)(2,1)S(1)} all-to-all(bf16[8,1,6,4096]{3,2,1,0:T(8,128)(2,1)S(1)} %bitcast.129), channel_id=1, replica_groups=mesh['ctx'=16,'exp'=8,'dp'=2] {'exp'}, dimensions={0} | all-to-all | bytes 786432 | tf_op jit(solution)/shard_map/all_to_all | solution.py:134
  230.6 14.9 %pad_maximum_fusion = bf16[2,1,2048,2,512]{4,3,2,1,0:T(2,128)(2,1)} fusion(bf16[1,1,2048,2,512]{4,3,2,1,0:T(2,128)(2,1)} %bitcast.127), kind=kLoop, calls=%fused_computation.19 | loop fusion | flops 4194304 | bytes 12582912 | tf_op jit(solution)/shard_map/stack | solution.py:50
  245.5 7.0 %all-to-all-start = ((bf16[2,1,2048,2,512]{4,3,2,1,0:T(2,128)(2,1)}), bf16[2,1,2048,2,512]{4,3,2,1,0:T(2,128)(2,1)}, u32[]{:S(2)}, u32[]{:S(2)}) async-start(bf16[2,1,2048,2,512]{4,3,2,1,0:T(2,128)(2,1)} %pad_maximum_fusion), calls=%async_computation.1 | async-start | bytes 16777216 | tf_op jit(solution)/shard_map/all_to_all | solution.py:50
  253.4 134.7 %all-to-all-done = bf16[2,1,2048,2,512]{4,3,2,1,0:T(2,128)(2,1)} async-done(((bf16[2,1,2048,2,512]{4,3,2,1,0:T(2,128)(2,1)}), bf16[2,1,2048,2,512]{4,3,2,1,0:T(2,128)(2,1)}, u32[]{:S(2)}, u32[]{:S(2)}) %all-to-all-start) | async-done | bytes 8388640 | tf_op jit(solution)/shard_map/all_to_all | solution.py:50
  388.1 8.0 %copy.52 = bf16[2,1,2048,2,512]{4,2,0,3,1:T(8,128)(2,1)} copy(bf16[2,1,2048,2,512]{4,3,2,1,0:T(2,128)(2,1)} %all-to-all-done) | data formatting | bytes 16777216 | tf_op jit(solution)/shard_map/all_to_all | solution.py:50
  396.1 11.5 %fusion.30 = f32[16,8,1,6,2,512]{5,0,3,1,4,2:T(8,128)S(1)} fusion(bf16[4096,2,512,1,1]{2,0,4,3,1:T(8,128)(2,1)} %bitcast.126, bf16[16,8,6,4096]{3,1,0,2:T(8,128)(2,1)} %bitcast.137), kind=kOutput, calls=%fused_computation.39 | convolution fusion | flops 6442450944 | bytes 17825792 | tf_op jit(solution)/shard_map/cnlrd,ldjf->cnlrjf/dot_general | solution.py:136
  408.2 8.0 %fusion.22 = bf16[16,8,1,6,4096]{4,1,3,0,2:T(8,128)(2,1)} fusion(bf16[1,512,4096]{2,1,0:T(8,128)(2,1)} %all-gather.11.cloned.1.call-done, bf16[16,8,6,512]{3,0,2,1:T(8,128)(2,1)S(1)} %fusion.42), kind=kOutput, calls=%fused_computation.26 | convolution fusion | flops 3224371200 | bytes 11272192 | tf_op jit(solution)/shard_map/cnlrf,lfd->cnlrd/dot_general | solution.py:141
  416.2 93.7 %reduce-scatter.5.cloned.1.call-done = bf16[1,8,1,6,4096]{4,1,3,0,2:T(8,128)(2,1)} async-done(((bf16[16,8,1,6,4096]{4,1,3,0,2:T(8,128)(2,1)}), bf16[1,8,1,6,4096]{4,1,3,0,2:T(8,128)(2,1)}) %reduce-scatter.5.cloned.1.call-update) | async-done | bytes 393232 | tf_op jit(solution)/shard_map/reduce_scatter | solution.py:140
  509.9 2.0 copy.57
  511.9 7.0 %all-to-all-start.2 = ((bf16[8,1,6,4096]{3,2,1,0:T(8,128)(2,1)}), bf16[8,1,6,4096]{3,2,1,0:T(8,128)(2,1)S(1)}, u32[]{:S(2)}, u32[]{:S(2)}) async-start(bf16[8,1,6,4096]{3,2,1,0:T(8,128)(2,1)} %copy.57), calls=%async_computation.4 | async-start | bytes 1048576 | tf_op jit(solution)/shard_map/all_to_all | solution.py:149
  519.2 16.1 %all-to-all-done.2 = bf16[8,1,6,4096]{3,2,1,0:T(8,128)(2,1)S(1)} async-done(((bf16[8,1,6,4096]{3,2,1,0:T(8,128)(2,1)}), bf16[8,1,6,4096]{3,2,1,0:T(8,128)(2,1)S(1)}, u32[]{:S(2)}, u32[]{:S(2)}) %all-to-all-start.2) | async-done | bytes 393248 | tf_op jit(solution)/shard_map/all_to_all | solution.py:149
  535.4 1.0 fusion.25
  (56 shorter events, 6.2 us)
Async XLA Ops:
  6.5 512.4 %copy-start = (bf16[4096,8]{0,1:T(8,128)(2,1)S(1)}, bf16[4096,8]{0,1:T(8,128)(2,1)}, u32[]{:S(2)}) copy-start(bf16[4096,8]{0,1:T(8,128)(2,1)} %param.17) | copy-start | bytes 196612
  6.5 93.4 %all-gather.7.cloned.1.call-start = ((), (), s32[]{:S(2)}) async-start(), calls=%async_computation.5 | async-start | bytes 9437184 | tf_op jit(solution)/shard_map/all_gather | solution.py:47
  11.3 0.8 copy-start.2
  11.3 1.2 copy-start.1
  11.4 153.2 %all-gather.9.cloned.1.call-start = ((), (), s32[]{:S(2)}) async-start(), calls=%async_computation.6 | async-start | bytes 6291456 | tf_op jit(solution)/shard_map/all_gather | solution.py:48
  12.1 198.3 %reduce-scatter.3.cloned.1.call-start = ((), (), s32[]{:S(2)}) async-start(), calls=%async_computation.7 | async-start | bytes 1179648 | tf_op jit(solution)/shard_map/reduce_scatter | solution.py:108
  154.5 14.1 %copy-start.3 = (bf16[4096]{0:T(1024)(128)(2,1)S(1)}, bf16[4096]{0:T(1024)(128)(2,1)}, u32[]{:S(2)}) copy-start(bf16[4096]{0:T(1024)(128)(2,1)} %param.16) | copy-start | bytes 24580
  154.6 14.1 %copy-start.4 = (s32[1,16,2]{1,2,0:T(2,128)S(1)}, s32[1,16,2]{1,2,0:T(2,128)}, u32[]{:S(2)}) copy-start(s32[1,16,2]{1,2,0:T(2,128)} %param.20) | copy-start | bytes 388
  154.6 14.1 %copy-start.5 = (s32[1,16,2]{1,2,0:T(2,128)S(1)}, s32[1,16,2]{1,2,0:T(2,128)}, u32[]{:S(2)}) copy-start(s32[1,16,2]{1,2,0:T(2,128)} %param.21) | copy-start | bytes 388
  168.5 227.6 %all-gather.13.cloned.1.call-start = ((), (), s32[]{:S(2)}) async-start(), calls=%async_computation.10 | async-start | bytes 6684672 | tf_op jit(solution)/shard_map/all_gather | solution.py:135
  245.5 142.5 %all-to-all-start = ((bf16[2,1,2048,2,512]{4,3,2,1,0:T(2,128)(2,1)}), bf16[2,1,2048,2,512]{4,3,2,1,0:T(2,128)(2,1)}, u32[]{:S(2)}, u32[]{:S(2)}) async-start(bf16[2,1,2048,2,512]{4,3,2,1,0:T(2,128)(2,1)} %pad_maximum_fusion), calls=%async_computation.1 | async-start | bytes 16777216 | tf_op jit(solution)/shard_map/all_to_all | solution.py:50
  252.5 155.6 %all-gather.11.cloned.1.call-start = ((), (), s32[]{:S(2)}) async-start(), calls=%async_computation.8 | async-start | bytes 6291456 | tf_op jit(solution)/shard_map/all_gather | solution.py:52
  253.1 256.8 %reduce-scatter.5.cloned.1.call-start = ((), (), s32[]{:S(2)}) async-start(), calls=%async_computation.9 | async-start | bytes 6684672 | tf_op jit(solution)/shard_map/reduce_scatter | solution.py:140
  511.9 23.3 %all-to-all-start.2 = ((bf16[8,1,6,4096]{3,2,1,0:T(8,128)(2,1)}), bf16[8,1,6,4096]{3,2,1,0:T(8,128)(2,1)S(1)}, u32[]{:S(2)}, u32[]{:S(2)}) async-start(bf16[8,1,6,4096]{3,2,1,0:T(8,128)(2,1)} %copy.57), calls=%async_computation.4 | async-start | bytes 1048576 | tf_op jit(solution)/shard_map/all_to_all | solution.py:149
Sparse Core Ops, SparseCore 0:
  11.5 88.4 all-gather.6
  101.7 62.8 all-gather.8
  168.7 41.7 reduce-scatter.2
  230.8 82.8 all-gather.12
  315.3 85.9 all-gather.10
  416.4 93.5 reduce-scatter.4
